TPU v7x, 32 devices: a whole 2x2x4 slice. The times are simulated.
32 devices in a mesh: groups: 2 (over y), space: 4 (over z), tangent: 4 (over x, core).
Axes of the slice: x: 2, y: 2, z: 4, core: 2. Of those that a mesh axis runs over, the one named last changes fastest.
Arguments:
- positions: float32 [16, 2, 128], P(('groups', 'space')), parts along dimension 0, may hold values from 0.45 to 15.55, as said below
- momenta: float32 [16, 2, 128], P(('groups', 'space')), parts along dimension 0, may hold values from -4 to 4
- cell_count: int32 [16], P(('groups', 'space')), parts along dimension 0, may hold values from 64 to 128, as said below
- tangent: float32 [16, 4, 128, 1024], P(('groups', 'space'), None, None, 'tangent'), parts along dimension 0, may hold values from -6 to 6
Outputs:
- phase: float32 [16, 4, 128], P(('groups', 'space')), parts along dimension 0
- new_tangent: float32 [16, 4, 128, 1024], P(('groups', 'space'), None, None, 'tangent'), parts along dimension 0
- stretch: float32 [2048], P(('groups', 'tangent')), parts along dimension 0
There are 2 independent parts, one for each index of `groups`. A program takes and returns all parts, laid end to end along the dimension named above; each array names one. Nothing has to cross between parts.
Inputs may be any that keep to these rules, and one draw needn't show every extreme that they name: Slots 0 to cell_count - 1 of a cell hold particles, the others are padding; some cell holds 128 particles in every draw. `positions`: every slot of a cell, padding too, lies within 0.05 in each coordinate of its own point of the lattice (m + 0.5, n + 0.5), m from 0 to 7, n from 0 to 15; no two slots of a cell share a lattice point.
All inputs are finite; a program needn't handle non-finite values.
Results may differ from a plain program's by a relative error of at most 0.006.
Values may be sent and summed in bfloat16 or wider, within the bound.
No kernel may reach another device: no remote copies, remote signals or barrier semaphores. Data moves between devices by JAX's collectives and lax.ppermute only.
A program may use at most 128 MiB of HBM per device.

v0:
```python
import jax
import jax.numpy as jnp
from jax import lax
from jax.sharding import PartitionSpec as P

STEPS = 2
DT = 0.005
CUT2 = 2.0 ** (1.0 / 3.0)
PARK = 1000.0
HIGH = lax.Precision.HIGHEST


def padded(block, sides, width):
    for axis, dim in sides:
        count = lax.axis_size(axis)
        forward = [(i, i + 1) for i in range(count - 1)]
        forward.append((count - 1, 0))
        backward = [(target, source) for source, target in forward]
        low = lax.ppermute(
            lax.slice_in_dim(block, block.shape[dim] - width, None, axis=dim), axis, forward
        )
        high = lax.ppermute(lax.slice_in_dim(block, 0, width, axis=dim), axis, backward)
        block = jnp.concatenate([low, block, high], axis=dim)
    return block


def pair_terms(own_coords, own_alive, far_coords, shift_x, shift_y, same_cell):
    delta_x = shift_x + far_coords[:, 0, None, :] - own_coords[:, 0, :, None]
    delta_y = shift_y + far_coords[:, 1, None, :] - own_coords[:, 1, :, None]
    dist2 = delta_x * delta_x + delta_y * delta_y
    within = jnp.logical_and(dist2 < CUT2, own_alive[:, :, None] > 0.5)
    if same_cell:
        within = jnp.logical_and(within, jnp.logical_not(jnp.eye(dist2.shape[-1], dtype=bool)))
    weight = within.astype(jnp.float32)
    safe = jnp.where(within, dist2, CUT2)
    inverse = 1.0 / safe
    inv_three = inverse * inverse * inverse
    inv_six = inv_three * inv_three
    energy = 4.0 * (inv_six - inv_three) + 1.0
    energy_1 = 4.0 * (3.0 * inv_three - 6.0 * inv_six) * inverse
    energy_2 = 4.0 * (42.0 * inv_six - 12.0 * inv_three) * inverse * inverse
    taper = 1.0 - safe / CUT2
    switch = taper * taper
    switch_1 = -2.0 * taper / CUT2
    switch_2 = 2.0 / (CUT2 * CUT2)
    grad_1 = (energy_1 * switch + energy * switch_1) * weight
    grad_2 = (energy_2 * switch + 2.0 * energy_1 * switch_1 + energy * switch_2) * weight
    pull_x = 2.0 * grad_1 * delta_x
    pull_y = 2.0 * grad_1 * delta_y
    k_xx = (2.0 * grad_1 + 4.0 * grad_2 * delta_x * delta_x).astype(jnp.bfloat16)
    k_xy = (4.0 * grad_2 * delta_x * delta_y).astype(jnp.bfloat16)
    k_yy = (2.0 * grad_1 + 4.0 * grad_2 * delta_y * delta_y).astype(jnp.bfloat16)
    return (pull_x, pull_y, k_xx, k_xy, k_yy)


def apply_rows(k_xx, k_xy, k_yy, far_low):
    gain_x = jnp.einsum(
        "cij,cjv->civ", k_xx, far_low[:, 0], preferred_element_type=jnp.float32
    ) + jnp.einsum("cij,cjv->civ", k_xy, far_low[:, 1], preferred_element_type=jnp.float32)
    gain_y = jnp.einsum(
        "cij,cjv->civ", k_xy, far_low[:, 0], preferred_element_type=jnp.float32
    ) + jnp.einsum("cij,cjv->civ", k_yy, far_low[:, 1], preferred_element_type=jnp.float32)
    return (gain_x, gain_y)


def add_pair(totals, parked, occupied, far_coords, far_low, shift_x, shift_y, same_cell):
    forces_x, forces_y, push_x, push_y, diag_xx, diag_xy, diag_yy = totals
    pull_x, pull_y, k_xx, k_xy, k_yy = pair_terms(
        parked, occupied, far_coords, shift_x, shift_y, same_cell
    )
    gain_x, gain_y = apply_rows(k_xx, k_xy, k_yy, far_low)
    totals = (
        forces_x + jnp.sum(pull_x, axis=2),
        forces_y + jnp.sum(pull_y, axis=2),
        push_x + gain_x,
        push_y + gain_y,
        diag_xx + jnp.sum(k_xx.astype(jnp.float32), axis=2),
        diag_xy + jnp.sum(k_xy.astype(jnp.float32), axis=2),
        diag_yy + jnp.sum(k_yy.astype(jnp.float32), axis=2),
    )
    return (totals, (pull_x, pull_y, k_xx, k_xy, k_yy))


def evaluate(coords, occupied, small_q):
    cell_total = coords.shape[0]
    low = small_q.astype(jnp.bfloat16)
    parked = jnp.concatenate(
        [coords[:, 0:1] + PARK * (1.0 - occupied)[:, None, :], coords[:, 1:2]], axis=1
    )
    empty_rows = jnp.zeros(occupied.shape, jnp.float32)
    empty_push = jnp.zeros(small_q[:, 0].shape, jnp.float32)
    totals = (empty_rows, empty_rows, empty_push, empty_push, empty_rows, empty_rows, empty_rows)
    far_low = padded(low, (("space", 0),), cell_total)
    far_coords = padded(parked, (("space", 0),), cell_total)
    for side in (-1, 0, 1):
        if side == 0:
            block_low = low
            block_coords = parked
        else:
            begin = (1 + side) * cell_total
            block_low = far_low[begin : begin + cell_total]
            block_coords = far_coords[begin : begin + cell_total]
        for lane in (-1, 0, 1):
            totals, unused = add_pair(
                totals,
                parked,
                occupied,
                jnp.roll(block_coords, -lane, axis=0),
                jnp.roll(block_low, -lane, axis=0),
                8.0 * side,
                16.0 * lane,
                side == 0 and lane == 0,
            )
    forces_x, forces_y, push_x, push_y, diag_xx, diag_xy, diag_yy = totals
    wide_own = low.astype(jnp.float32)
    push_x = push_x - diag_xx[..., None] * wide_own[:, 0] - diag_xy[..., None] * wide_own[:, 1]
    push_y = push_y - diag_xy[..., None] * wide_own[:, 0] - diag_yy[..., None] * wide_own[:, 1]
    forces = jnp.stack([forces_x, forces_y], axis=1)
    pushes = jnp.stack([push_x, push_y], axis=1)
    return (forces, pushes)


def body(positions, momenta, cell_count, tangent):
    cell_total = positions.shape[0]
    slot_count = positions.shape[2]
    block_cols = tangent.shape[3]
    occupied = (
        lax.broadcasted_iota(jnp.int32, (cell_total, slot_count), 1) < cell_count[:, None]
    ).astype(jnp.float32)
    state = tangent * occupied[:, None, :, None]
    coords = positions
    speeds = momenta
    small_q = state[:, 0:2]
    small_p = state[:, 2:4]
    forces, pushes = evaluate(coords, occupied, small_q)
    for step_index in range(STEPS):
        midway_p = speeds + 0.5 * DT * forces
        midway_dp = small_p + 0.5 * DT * pushes
        coords = coords + DT * midway_p
        small_q = small_q + DT * midway_dp
        forces, pushes = evaluate(coords, occupied, small_q)
        speeds = midway_p + 0.5 * DT * forces
        small_p = midway_dp + 0.5 * DT * pushes
    phase = jnp.concatenate([coords, speeds], axis=1)
    final = jnp.concatenate([small_q, small_p], axis=1)
    rows_form = lax.all_to_all(final, "tangent", split_axis=2, concat_axis=3, tiled=True)
    full_width = rows_form.shape[3]
    flat_rows = rows_form.reshape(-1, full_width)
    partial_value = lax.dot_general(
        flat_rows,
        flat_rows,
        (((0,), (0,)), ((), ())),
        precision=HIGH,
        preferred_element_type=jnp.float32,
    )
    gram_scale = 1.0 / (4.0 * slot_count * cell_total * lax.axis_size("space"))
    gram = lax.psum(partial_value, ("space", "tangent"))
    factor = jnp.linalg.cholesky(gram * gram_scale)
    solved = jax.scipy.linalg.solve_triangular(factor, flat_rows.T, lower=True).T
    columns_out = lax.all_to_all(
        solved.reshape(rows_form.shape), "tangent", split_axis=3, concat_axis=2, tiled=True
    )
    log_diag = jnp.log(jnp.diagonal(factor))
    stretch = lax.dynamic_slice_in_dim(log_diag, lax.axis_index("tangent") * block_cols, block_cols)
    return (phase, columns_out, stretch)


def solution(mesh):
    placed = (
        P(("groups", "space"), None, None),
        P(("groups", "space"), None, None),
        P(("groups", "space")),
        P(("groups", "space"), None, None, "tangent"),
    )
    return jax.shard_map(
        body,
        mesh=mesh,
        in_specs=placed,
        out_specs=(
            P(("groups", "space"), None, None),
            P(("groups", "space"), None, None, "tangent"),
            P(("groups", "tangent")),
        ),
        check_vma=False,
    )
```

profile of v0, /device:TPU:1, one launch (start us, length us, event | category | flops | bytes accessed | tf_op | source)
XLA Modules:
  0.0 639.7 jit_solution(17771305510368086692)
XLA Ops:
  86.5 7.0 %collective-permute-done.10 = bf16[2,2,128,256]{3,2,0,1:T(8,128)(2,1)S(1)} collective-permute-done((bf16[2,2,128,256]{3,2,0,1:T(8,128)(2,1)S(1)}, bf16[2,2,128,256]{3,2,0,1:T(8,128)(2,1)S(1)}, u32[]{:S(2)}, u32[]{:S(2)}) %collective-permute-start.10) | collective-permute-done | bytes 262176 | tf_op jit(solution)/shard_map/ppermute | solution.py:19
  105.5 21.8 %all_to_all.33 = f32[2,4,128,256]{3,0,1,2:T(2,128)S(1)} all-to-all(f32[2,4,128,256]{3,0,1,2:T(2,128)S(1)} %copy.18), channel_id=1, replica_groups=mesh['groups'=2,'space'=4,'tangent'=4] {'tangent'}, dimensions={2} | all-to-all | bytes 2097152 | tf_op jit(solution)/shard_map/all_to_all | solution.py:146
  133.8 107.8 %all-reduce.3.cloned.1.call-done = f32[1024,1024]{0,1:T(8,128)} async-done(((f32[1024,1024]{0,1:T(8,128)}), f32[1024,1024]{0,1:T(8,128)}) %all-reduce.3.cloned.1.call-update) | async-done | bytes 4194320 | tf_op jit(solution)/shard_map/psum | solution.py:157
  246.6 5.7 copy.21
  258.7 11.7 %cholesky.187 = f32[128,128]{1,0:T(8,128)S(1)} custom-call(f32[128,128]{1,0:T(8,128)S(1)} %cholesky.514), custom_call_target="Cholesky" | custom-call | tf_op jit(solution)/shard_map/jit(cholesky)/cholesky | solution.py:158
  271.1 9.8 %custom-call.63 = f32[1,128,128]{1,2,0:T(8,128)S(1)} custom-call(f32[1,128,128]{2,1,0:T(8,128)S(1)} %get-tuple-element.432), custom_call_target="InvertDiagBlocksLowerTriangular" | custom-call | tf_op jit(solution)/shard_map/jit(cholesky)/cholesky | solution.py:158
  287.3 11.9 %cholesky.209 = f32[128,128]{1,0:T(8,128)S(1)} custom-call(f32[128,128]{1,0:T(8,128)S(1)} %cholesky.518), custom_call_target="Cholesky" | custom-call | tf_op jit(solution)/shard_map/jit(cholesky)/cholesky | solution.py:158
  300.5 9.8 %custom-call.64 = f32[1,128,128]{1,2,0:T(8,128)S(1)} custom-call(f32[1,128,128]{2,1,0:T(8,128)S(1)} %get-tuple-element.429), custom_call_target="InvertDiagBlocksLowerTriangular" | custom-call | tf_op jit(solution)/shard_map/jit(cholesky)/cholesky | solution.py:158
  313.6 11.7 %cholesky.402 = f32[128,128]{1,0:T(8,128)S(1)} custom-call(f32[128,128]{1,0:T(8,128)S(1)} %cholesky.523), custom_call_target="Cholesky" | custom-call | tf_op jit(solution)/shard_map/jit(cholesky)/cholesky | solution.py:158
  326.6 9.8 %custom-call.65 = f32[1,128,128]{1,2,0:T(8,128)S(1)} custom-call(f32[1,128,128]{2,1,0:T(8,128)S(1)} %get-tuple-element.426), custom_call_target="InvertDiagBlocksLowerTriangular" | custom-call | tf_op jit(solution)/shard_map/jit(cholesky)/cholesky | solution.py:158
  340.0 11.9 %cholesky.421 = f32[128,128]{1,0:T(8,128)S(1)} custom-call(f32[128,128]{1,0:T(8,128)S(1)} %cholesky.528), custom_call_target="Cholesky" | custom-call | tf_op jit(solution)/shard_map/jit(cholesky)/cholesky | solution.py:158
  353.3 9.8 %custom-call.66 = f32[1,128,128]{1,2,0:T(8,128)S(1)} custom-call(f32[1,128,128]{2,1,0:T(8,128)S(1)} %get-tuple-element.423), custom_call_target="InvertDiagBlocksLowerTriangular" | custom-call | tf_op jit(solution)/shard_map/jit(cholesky)/cholesky | solution.py:158
  366.5 11.7 %cholesky.440 = f32[128,128]{1,0:T(8,128)S(1)} custom-call(f32[128,128]{1,0:T(8,128)S(1)} %cholesky.533), custom_call_target="Cholesky" | custom-call | tf_op jit(solution)/shard_map/jit(cholesky)/cholesky | solution.py:158
  379.6 10.2 %custom-call.67 = f32[1,128,128]{1,2,0:T(8,128)S(1)} custom-call(f32[1,128,128]{2,1,0:T(8,128)S(1)} %get-tuple-element.420), custom_call_target="InvertDiagBlocksLowerTriangular" | custom-call | tf_op jit(solution)/shard_map/jit(cholesky)/cholesky | solution.py:158
  393.1 11.7 %cholesky.460 = f32[128,128]{1,0:T(8,128)S(1)} custom-call(f32[128,128]{1,0:T(8,128)S(1)} %cholesky.538), custom_call_target="Cholesky" | custom-call | tf_op jit(solution)/shard_map/jit(cholesky)/cholesky | solution.py:158
  406.1 9.8 %custom-call.68 = f32[1,128,128]{1,2,0:T(8,128)S(1)} custom-call(f32[1,128,128]{2,1,0:T(8,128)S(1)} %get-tuple-element.417), custom_call_target="InvertDiagBlocksLowerTriangular" | custom-call | tf_op jit(solution)/shard_map/jit(cholesky)/cholesky | solution.py:158
  418.9 11.9 %cholesky.480 = f32[128,128]{1,0:T(8,128)S(1)} custom-call(f32[128,128]{1,0:T(8,128)S(1)} %cholesky.543), custom_call_target="Cholesky" | custom-call | tf_op jit(solution)/shard_map/jit(cholesky)/cholesky | solution.py:158
  432.1 9.8 %custom-call.69 = f32[1,128,128]{1,2,0:T(8,128)S(1)} custom-call(f32[1,128,128]{2,1,0:T(8,128)S(1)} %get-tuple-element.414), custom_call_target="InvertDiagBlocksLowerTriangular" | custom-call | tf_op jit(solution)/shard_map/jit(cholesky)/cholesky | solution.py:158
  444.5 11.7 %cholesky.498 = f32[128,128]{1,0:T(8,128)S(1)} custom-call(f32[128,128]{1,0:T(8,128)S(1)} %convolution_subtract_fusion.13), custom_call_target="Cholesky" | custom-call | tf_op jit(solution)/shard_map/jit(cholesky)/cholesky | solution.py:158
  462.6 6.6 %fusion.1 = (f32[1024,1024]{1,0:T(8,128)}, f32[1024,1024]{1,0:T(8,128)}) fusion(f32[1024,1024]{1,0:T(8,128)} %get-tuple-element.412, pred[]{:T(512)S(6)} %cholesky.513), kind=kLoop, calls=%fused_computation.7 | loop fusion | flops 4194304 | bytes 12582913 | tf_op jit(solution)/shard_map/jit(_solve_triangular)/triangular_solve | solution.py:159
  469.2 23.2 %while.1 = (s32[]{:T(128)}, f32[1024,1024]{1,0:T(8,128)}, s32[8,2]{0,1:T(2,128)S(1)}, f32[8,128,128]{2,1,0:T(8,128)S(1)}, s32[]{:T(128)}) while((s32[]{:T(128)}, f32[1024,1024]{1,0:T(8,128)}, s32[8,2]{0,1:T(2,128)S(1)}, f32[8,128,128]{2,1,0:T(8,128)S(1)}, s32[]{:T(128)}) %tuple.396), condition=%wide.while_cond, body=%wide.while_body.sunk | while | flops 2 | bytes 131189 | solution.py:159
  492.4 79.4 %custom-call.70 = f32[8,128,128]{1,2,0:T(8,128)} custom-call(f32[8,128,128]{2,1,0:T(8,128)S(1)} %get-tuple-element.10), custom_call_target="InvertDiagBlocksLowerTriangular" | custom-call | tf_op jit(solution)/shard_map/jit(_solve_triangular)/triangular_solve | solution.py:159
  595.5 5.5 all-to-all-start.1
  601.7 17.3 %gather_fusion = f32[1024]{0:T(1024)S(1)} fusion(f32[1024,1024]{1,0:T(8,128)} %get-tuple-element.320, s32[1024]{0:T(1024)S(1)} %bitcast.397), kind=kCustom, calls=%fused_computation | custom fusion | bytes 16384 | tf_op jit(solution)/shard_map/jit(diagonal)/cond/branch_0_fun/gather | solution.py:163
  (326 shorter events, 204.9 us)
Async XLA Ops:
  7.2 234.4 %all-reduce.3.cloned.1.call-start = ((), (), s32[]{:S(2)}) async-start(), calls=%async_computation.2 | async-start | bytes 8388608 | tf_op jit(solution)/shard_map/psum | solution.py:157
  8.1 12.2 %collective-permute-start.1 = (f32[2,2,128]{2,1,0:T(2,128)S(1)}, f32[2,2,128]{2,1,0:T(2,128)S(1)}, u32[]{:S(2)}, u32[]{:S(2)}) collective-permute-start(f32[2,2,128]{2,1,0:T(2,128)S(1)} %pad_maximum_fusion.11), channel_id=1, source_target_pairs={{4,0},{8,4},{12,8},{0,12},{5,1},{9,5},{13,9},{1,13},{6,2},{10,6},{... | collective-permute-start | bytes 6152 | tf_op jit(solution)/shard_map/ppermute | solution.py:22
  12.3 8.1 %collective-permute-start = (f32[2,2,128]{2,1,0:T(2,128)S(1)}, f32[2,2,128]{2,1,0:T(2,128)S(1)}, u32[]{:S(2)}, u32[]{:S(2)}) collective-permute-start(f32[2,2,128]{2,1,0:T(2,128)S(1)} %pad_maximum_fusion.11), channel_id=1, source_target_pairs={{0,4},{4,8},{8,12},{12,0},{1,5},{5,9},{9,13},{13,1},{2,6},{6,10},{... | collective-permute-start | bytes 6152 | tf_op jit(solution)/shard_map/ppermute | solution.py:19
  14.4 28.2 %collective-permute-start.7 = (bf16[2,2,128,256]{3,2,0,1:T(8,128)(2,1)S(1)}, bf16[2,2,128,256]{3,2,0,1:T(8,128)(2,1)S(1)}, u32[]{:S(2)}, u32[]{:S(2)}) collective-permute-start(bf16[2,2,128,256]{3,2,0,1:T(8,128)(2,1)S(1)} %get-tuple-element.327), channel_id=1, source_target_pairs={{4,0},{8,4},{12,8},{0,12},{5,1},{9,5},{13,9},{1,13},{6,2},{10,6},{... | collective-permute-start | bytes 786440 | tf_op jit(solution)/shard_map/ppermute | solution.py:22
  17.7 26.6 %collective-permute-start.6 = (bf16[2,2,128,256]{3,2,0,1:T(8,128)(2,1)S(1)}, bf16[2,2,128,256]{3,2,0,1:T(8,128)(2,1)S(1)}, u32[]{:S(2)}, u32[]{:S(2)}) collective-permute-start(bf16[2,2,128,256]{3,2,0,1:T(8,128)(2,1)S(1)} %get-tuple-element.327), channel_id=1, source_target_pairs={{0,4},{4,8},{8,12},{12,0},{1,5},{5,9},{9,13},{13,1},{2,6},{6,10},{... | collective-permute-start | bytes 786440 | tf_op jit(solution)/shard_map/ppermute | solution.py:19
  18.6 4.9 copy-start.3
  18.6 4.9 copy-start.4
  18.7 4.9 copy-start.2
  23.7 4.2 collective-permute-start.3
  27.0 4.2 collective-permute-start.2
  34.6 2.5 collective-permute-start.5
  35.0 4.2 collective-permute-start.4
  57.1 7.5 %collective-permute-start.9 = (bf16[2,2,128,256]{3,2,0,1:T(8,128)(2,1)S(1)}, bf16[2,2,128,256]{3,2,0,1:T(8,128)(2,1)S(1)}, u32[]{:S(2)}, u32[]{:S(2)}) collective-permute-start(bf16[2,2,128,256]{3,2,0,1:T(8,128)(2,1)S(1)} %get-tuple-element.325), channel_id=1, source_target_pairs={{4,0},{8,4},{12,8},{0,12},{5,1},{9,5},{13,9},{1,13},{6,2},{10,6},{... | collective-permute-start | bytes 786440 | tf_op jit(solution)/shard_map/ppermute | solution.py:22
  58.0 8.5 %collective-permute-start.8 = (bf16[2,2,128,256]{3,2,0,1:T(8,128)(2,1)S(1)}, bf16[2,2,128,256]{3,2,0,1:T(8,128)(2,1)S(1)}, u32[]{:S(2)}, u32[]{:S(2)}) collective-permute-start(bf16[2,2,128,256]{3,2,0,1:T(8,128)(2,1)S(1)} %get-tuple-element.325), channel_id=1, source_target_pairs={{0,4},{4,8},{8,12},{12,0},{1,5},{5,9},{9,13},{13,1},{2,6},{6,10},{... | collective-permute-start | bytes 786440 | tf_op jit(solution)/shard_map/ppermute | solution.py:19
  79.4 5.5 collective-permute-start.11
  80.8 12.8 %collective-permute-start.10 = (bf16[2,2,128,256]{3,2,0,1:T(8,128)(2,1)S(1)}, bf16[2,2,128,256]{3,2,0,1:T(8,128)(2,1)S(1)}, u32[]{:S(2)}, u32[]{:S(2)}) collective-permute-start(bf16[2,2,128,256]{3,2,0,1:T(8,128)(2,1)S(1)} %get-tuple-element.322), channel_id=1, source_target_pairs={{0,4},{4,8},{8,12},{12,0},{1,5},{5,9},{9,13},{13,1},{2,6},{6,10},{... | collective-permute-start | bytes 786440 | tf_op jit(solution)/shard_map/ppermute | solution.py:19
  256.8 1.9 copy-start
  571.8 7.2 %copy-start.1 = (f32[8,128,128]{1,2,0:T(8,128)S(1)}, f32[8,128,128]{1,2,0:T(8,128)}, u32[]{:S(2)}) copy-start(f32[8,128,128]{1,2,0:T(8,128)} %custom-call.70) | copy-start | bytes 1572868
  595.5 24.2 %all-to-all-start.1 = ((f32[4,1,65536]{2,1,0:T(1,128)}), f32[4,1,65536]{2,1,0:T(1,128)S(1)}, u32[]{:S(2)}, u32[]{:S(2)}) async-start(f32[4,1,65536]{2,1,0:T(1,128)} %reshape.847), calls=%async_computation.1 | async-start | bytes 2097152 | tf_op jit(solution)/shard_map/all_to_all | solution.py:160
Sparse Core Ops, SparseCore 0:
  133.6 107.9 all-reduce.2
where the time goes:
time: 647 us; the launch traced here: 640 us
  other arithmetic  287 us (44%)
  waiting for transfers between devices  130 us (20%)
  matrix products  87.6 us (14%)
  local copies, waits for them, and re-layouts  71.5 us (11%)
  starting transfers between devices  21.9 us (3%)
  blocking collectives  21.8 us (3%)
  between operations  20.3 us (3%)
    another operation x31, other arithmetic, body(): factor = jnp.linalg.cholesky(gram * gram_scale)  173 us
    psum x1, waiting for transfers between devices, body(): gram = lax.psum(partial_value, ('space', 'tangent'))  108 us
    another operation x3, other arithmetic, body(): jax.scipy.linalg.solve_triangular(factor, flat_rows.T, lower=True)  86 us
    another operation x14, matrix products, body(): factor = jnp.linalg.cholesky(gram * gram_scale)  23.1 us
    another operation x24, local copies, waits for them, and re-layouts  23 us
    all_to_all x1, blocking collectives, body(): lax.all_to_all(final, 'tangent', split_axis=2, concat_axis=3, tiled=True)  21.8 us
    gather x1, local copies, waits for them, and re-layouts, body(): log_diag = jnp.log(jnp.diagonal(factor))  17.3 us
    another operation x15, matrix products, body(): jax.scipy.linalg.solve_triangular(factor, flat_rows.T, lower=True)  14.7 us
  transfers between devices with their start and end apart: 14, of which 9 were waited for; matrix products, arithmetic and copies ran while one was open for 6% of the time, Pallas kernels for 0%

commit v1 on v0

--- a/solution.py
+++ b/solution.py
@@ -1,3 +1,4 @@
+import functools
 import jax
 import jax.numpy as jnp
 from jax import lax
@@ -8,6 +9,13 @@
 CUT2 = 2.0 ** (1.0 / 3.0)
 PARK = 1000.0
 HIGH = lax.Precision.HIGHEST
+
+
+def domain_enter(frame_in, device_axis, across):
+    return lax.psum(lax.psum(frame_in, device_axis), across)
+
+
+follow_the_zone = functools.partial(domain_enter, device_axis="tangent", across="space")
 
 
 def padded(block, sides, width):
@@ -154,7 +162,7 @@
         preferred_element_type=jnp.float32,
     )
     gram_scale = 1.0 / (4.0 * slot_count * cell_total * lax.axis_size("space"))
-    gram = lax.psum(partial_value, ("space", "tangent"))
+    gram = follow_the_zone(partial_value)
     factor = jnp.linalg.cholesky(gram * gram_scale)
     solved = jax.scipy.linalg.solve_triangular(factor, flat_rows.T, lower=True).T
     columns_out = lax.all_to_all(

time: 647 us -> 775 us (1.20)
  waiting for transfers between devices: 130 us -> 263 us
    psum x1 -> x2, waiting for transfers between devices: 108 us -> 240 us  [domain_enter(): return lax.psum(lax.psum(frame_in, device_axis), across)]
  transfers between devices with their start and end apart: 14 -> 15, of which waited for: 9 -> 10; matrix products, arithmetic and copies ran while one was open for 6% -> 5% of each run, Pallas kernels for 0% -> 0%
where the time goes in v1:
time: 775 us; the launch traced here: 768 us
  other arithmetic  286 us (37%)
  waiting for transfers between devices  263 us (34%)
  matrix products  84.9 us (11%)
  local copies, waits for them, and re-layouts  71.5 us (9%)
  blocking collectives  21.8 us (3%)
  starting transfers between devices  20.8 us (3%)
  between operations  20.3 us (3%)
    psum x2, waiting for transfers between devices, domain_enter(): return lax.psum(lax.psum(frame_in, device_axis), across)  240 us
    another operation x31, other arithmetic, body(): factor = jnp.linalg.cholesky(gram * gram_scale)  173 us
    another operation x3, other arithmetic, body(): jax.scipy.linalg.solve_triangular(factor, flat_rows.T, lower=True)  85.4 us
    another operation x14, matrix products, body(): factor = jnp.linalg.cholesky(gram * gram_scale)  23.1 us
    another operation x24, local copies, waits for them, and re-layouts  23 us
    all_to_all x1, blocking collectives, body(): lax.all_to_all(final, 'tangent', split_axis=2, concat_axis=3, tiled=True)  21.8 us
    gather x1, local copies, waits for them, and re-layouts, body(): log_diag = jnp.log(jnp.diagonal(factor))  17.3 us
  transfers between devices with their start and end apart: 15, of which 10 were waited for; matrix products, arithmetic and copies ran while one was open for 5% of the time, Pallas kernels for 0%

profile of v1, /device:TPU:1, one launch (start us, length us, event | category | flops | bytes accessed | tf_op | source)
XLA Modules:
  0.0 768.2 jit_solution(7363150155849417776)
XLA Ops:
  86.5 7.0 collective-permute-done.10
  105.5 21.8 %all_to_all.33 = f32[2,4,128,256]{3,0,1,2:T(2,128)S(1)} all-to-all(f32[2,4,128,256]{3,0,1,2:T(2,128)S(1)} %copy.18), channel_id=1, replica_groups=mesh['groups'=2,'space'=4,'tangent'=4] {'tangent'}, dimensions={2} | all-to-all | bytes 2097152 | tf_op jit(solution)/shard_map/all_to_all | solution.py:154
  133.4 83.1 %all-reduce.4.cloned.1.call-done = f32[1024,1024]{0,1:T(8,128)} async-done(((f32[1024,1024]{0,1:T(8,128)}), f32[1024,1024]{0,1:T(8,128)}) %all-reduce.4.cloned.1.call-update) | async-done | bytes 4194320 | tf_op jit(solution)/shard_map/psum | solution.py:15
  216.9 157.4 %all-reduce.6.cloned.1.call-done = f32[1024,1024]{0,1:T(8,128)} async-done(((f32[1024,1024]{0,1:T(8,128)}), f32[1024,1024]{0,1:T(8,128)}) %all-reduce.6.cloned.1.call-update) | async-done | bytes 4194320 | tf_op jit(solution)/shard_map/psum | solution.py:15
  379.3 5.7 copy.21
  391.5 11.7 %cholesky.187 = f32[128,128]{1,0:T(8,128)S(1)} custom-call(f32[128,128]{1,0:T(8,128)S(1)} %cholesky.514), custom_call_target="Cholesky" | custom-call | tf_op jit(solution)/shard_map/jit(cholesky)/cholesky | solution.py:166
  403.8 9.8 %custom-call.63 = f32[1,128,128]{1,2,0:T(8,128)S(1)} custom-call(f32[1,128,128]{2,1,0:T(8,128)S(1)} %get-tuple-element.432), custom_call_target="InvertDiagBlocksLowerTriangular" | custom-call | tf_op jit(solution)/shard_map/jit(cholesky)/cholesky | solution.py:166
  420.1 11.9 %cholesky.209 = f32[128,128]{1,0:T(8,128)S(1)} custom-call(f32[128,128]{1,0:T(8,128)S(1)} %cholesky.518), custom_call_target="Cholesky" | custom-call | tf_op jit(solution)/shard_map/jit(cholesky)/cholesky | solution.py:166
  433.2 9.8 %custom-call.64 = f32[1,128,128]{1,2,0:T(8,128)S(1)} custom-call(f32[1,128,128]{2,1,0:T(8,128)S(1)} %get-tuple-element.429), custom_call_target="InvertDiagBlocksLowerTriangular" | custom-call | tf_op jit(solution)/shard_map/jit(cholesky)/cholesky | solution.py:166
  446.4 11.7 %cholesky.402 = f32[128,128]{1,0:T(8,128)S(1)} custom-call(f32[128,128]{1,0:T(8,128)S(1)} %cholesky.523), custom_call_target="Cholesky" | custom-call | tf_op jit(solution)/shard_map/jit(cholesky)/cholesky | solution.py:166
  459.4 9.8 %custom-call.65 = f32[1,128,128]{1,2,0:T(8,128)S(1)} custom-call(f32[1,128,128]{2,1,0:T(8,128)S(1)} %get-tuple-element.426), custom_call_target="InvertDiagBlocksLowerTriangular" | custom-call | tf_op jit(solution)/shard_map/jit(cholesky)/cholesky | solution.py:166
  472.8 11.9 %cholesky.421 = f32[128,128]{1,0:T(8,128)S(1)} custom-call(f32[128,128]{1,0:T(8,128)S(1)} %cholesky.528), custom_call_target="Cholesky" | custom-call | tf_op jit(solution)/shard_map/jit(cholesky)/cholesky | solution.py:166
  486.0 9.8 %custom-call.66 = f32[1,128,128]{1,2,0:T(8,128)S(1)} custom-call(f32[1,128,128]{2,1,0:T(8,128)S(1)} %get-tuple-element.423), custom_call_target="InvertDiagBlocksLowerTriangular" | custom-call | tf_op jit(solution)/shard_map/jit(cholesky)/cholesky | solution.py:166
  499.3 11.7 %cholesky.440 = f32[128,128]{1,0:T(8,128)S(1)} custom-call(f32[128,128]{1,0:T(8,128)S(1)} %cholesky.533), custom_call_target="Cholesky" | custom-call | tf_op jit(solution)/shard_map/jit(cholesky)/cholesky | solution.py:166
  512.4 10.2 %custom-call.67 = f32[1,128,128]{1,2,0:T(8,128)S(1)} custom-call(f32[1,128,128]{2,1,0:T(8,128)S(1)} %get-tuple-element.420), custom_call_target="InvertDiagBlocksLowerTriangular" | custom-call | tf_op jit(solution)/shard_map/jit(cholesky)/cholesky | solution.py:166
  525.9 11.7 %cholesky.460 = f32[128,128]{1,0:T(8,128)S(1)} custom-call(f32[128,128]{1,0:T(8,128)S(1)} %cholesky.538), custom_call_target="Cholesky" | custom-call | tf_op jit(solution)/shard_map/jit(cholesky)/cholesky | solution.py:166
  538.9 9.8 %custom-call.68 = f32[1,128,128]{1,2,0:T(8,128)S(1)} custom-call(f32[1,128,128]{2,1,0:T(8,128)S(1)} %get-tuple-element.417), custom_call_target="InvertDiagBlocksLowerTriangular" | custom-call | tf_op jit(solution)/shard_map/jit(cholesky)/cholesky | solution.py:166
  551.7 11.9 %cholesky.480 = f32[128,128]{1,0:T(8,128)S(1)} custom-call(f32[128,128]{1,0:T(8,128)S(1)} %cholesky.543), custom_call_target="Cholesky" | custom-call | tf_op jit(solution)/shard_map/jit(cholesky)/cholesky | solution.py:166
  564.8 9.8 %custom-call.69 = f32[1,128,128]{1,2,0:T(8,128)S(1)} custom-call(f32[1,128,128]{2,1,0:T(8,128)S(1)} %get-tuple-element.414), custom_call_target="InvertDiagBlocksLowerTriangular" | custom-call | tf_op jit(solution)/shard_map/jit(cholesky)/cholesky | solution.py:166
  577.3 11.7 %cholesky.498 = f32[128,128]{1,0:T(8,128)S(1)} custom-call(f32[128,128]{1,0:T(8,128)S(1)} %convolution_subtract_fusion.13), custom_call_target="Cholesky" | custom-call | tf_op jit(solution)/shard_map/jit(cholesky)/cholesky | solution.py:166
  595.3 6.6 fusion.1
  601.9 23.2 %while.1 = (s32[]{:T(128)}, f32[1024,1024]{1,0:T(8,128)}, s32[8,2]{0,1:T(2,128)S(1)}, f32[8,128,128]{2,1,0:T(8,128)S(1)}, s32[]{:T(128)}) while((s32[]{:T(128)}, f32[1024,1024]{1,0:T(8,128)}, s32[8,2]{0,1:T(2,128)S(1)}, f32[8,128,128]{2,1,0:T(8,128)S(1)}, s32[]{:T(128)}) %tuple.396), condition=%wide.while_cond, body=%wide.while_body.sunk | while | flops 2 | bytes 131189 | solution.py:167
  625.1 78.8 %custom-call.70 = f32[8,128,128]{1,2,0:T(8,128)S(1)} custom-call(f32[8,128,128]{2,1,0:T(8,128)S(1)} %get-tuple-element.10), custom_call_target="InvertDiagBlocksLowerTriangular" | custom-call | tf_op jit(solution)/shard_map/jit(_solve_triangular)/triangular_solve | solution.py:167
  730.1 17.3 %gather_fusion = f32[1024]{0:T(1024)S(1)} fusion(f32[1024,1024]{1,0:T(8,128)} %get-tuple-element.320, s32[1024]{0:T(1024)S(1)} %bitcast.397), kind=kCustom, calls=%fused_computation | custom fusion | bytes 16384 | tf_op jit(solution)/shard_map/jit(diagonal)/cond/branch_0_fun/gather | solution.py:171
  (327 shorter events, 206.8 us)
Async XLA Ops:
  7.2 209.4 %all-reduce.4.cloned.1.call-start = ((), (), s32[]{:S(2)}) async-start(), calls=%async_computation.2 | async-start | bytes 8388608 | tf_op jit(solution)/shard_map/psum | solution.py:15
  8.1 12.2 %collective-permute-start.1 = (f32[2,2,128]{2,1,0:T(2,128)S(1)}, f32[2,2,128]{2,1,0:T(2,128)S(1)}, u32[]{:S(2)}, u32[]{:S(2)}) collective-permute-start(f32[2,2,128]{2,1,0:T(2,128)S(1)} %pad_maximum_fusion.11), channel_id=1, source_target_pairs={{4,0},{8,4},{12,8},{0,12},{5,1},{9,5},{13,9},{1,13},{6,2},{10,6},{... | collective-permute-start | bytes 6152 | tf_op jit(solution)/shard_map/ppermute | solution.py:30
  12.3 8.1 %collective-permute-start = (f32[2,2,128]{2,1,0:T(2,128)S(1)}, f32[2,2,128]{2,1,0:T(2,128)S(1)}, u32[]{:S(2)}, u32[]{:S(2)}) collective-permute-start(f32[2,2,128]{2,1,0:T(2,128)S(1)} %pad_maximum_fusion.11), channel_id=1, source_target_pairs={{0,4},{4,8},{8,12},{12,0},{1,5},{5,9},{9,13},{13,1},{2,6},{6,10},{... | collective-permute-start | bytes 6152 | tf_op jit(solution)/shard_map/ppermute | solution.py:27
  14.4 28.2 %collective-permute-start.7 = (bf16[2,2,128,256]{3,2,0,1:T(8,128)(2,1)S(1)}, bf16[2,2,128,256]{3,2,0,1:T(8,128)(2,1)S(1)}, u32[]{:S(2)}, u32[]{:S(2)}) collective-permute-start(bf16[2,2,128,256]{3,2,0,1:T(8,128)(2,1)S(1)} %get-tuple-element.327), channel_id=1, source_target_pairs={{4,0},{8,4},{12,8},{0,12},{5,1},{9,5},{13,9},{1,13},{6,2},{10,6},{... | collective-permute-start | bytes 786440 | tf_op jit(solution)/shard_map/ppermute | solution.py:30
  17.7 26.6 %collective-permute-start.6 = (bf16[2,2,128,256]{3,2,0,1:T(8,128)(2,1)S(1)}, bf16[2,2,128,256]{3,2,0,1:T(8,128)(2,1)S(1)}, u32[]{:S(2)}, u32[]{:S(2)}) collective-permute-start(bf16[2,2,128,256]{3,2,0,1:T(8,128)(2,1)S(1)} %get-tuple-element.327), channel_id=1, source_target_pairs={{0,4},{4,8},{8,12},{12,0},{1,5},{5,9},{9,13},{13,1},{2,6},{6,10},{... | collective-permute-start | bytes 786440 | tf_op jit(solution)/shard_map/ppermute | solution.py:27
  18.6 4.9 copy-start.2
  18.6 4.9 copy-start.3
  18.7 4.9 copy-start.1
  23.7 4.2 collective-permute-start.3
  27.0 4.2 collective-permute-start.2
  34.6 2.5 collective-permute-start.5
  35.0 4.2 collective-permute-start.4
  57.1 7.5 collective-permute-start.9
  58.0 8.5 %collective-permute-start.8 = (bf16[2,2,128,256]{3,2,0,1:T(8,128)(2,1)S(1)}, bf16[2,2,128,256]{3,2,0,1:T(8,128)(2,1)S(1)}, u32[]{:S(2)}, u32[]{:S(2)}) collective-permute-start(bf16[2,2,128,256]{3,2,0,1:T(8,128)(2,1)S(1)} %get-tuple-element.325), channel_id=1, source_target_pairs={{0,4},{4,8},{8,12},{12,0},{1,5},{5,9},{9,13},{13,1},{2,6},{6,10},{... | collective-permute-start | bytes 786440 | tf_op jit(solution)/shard_map/ppermute | solution.py:27
  79.4 5.5 collective-permute-start.11
  80.8 12.8 %collective-permute-start.10 = (bf16[2,2,128,256]{3,2,0,1:T(8,128)(2,1)S(1)}, bf16[2,2,128,256]{3,2,0,1:T(8,128)(2,1)S(1)}, u32[]{:S(2)}, u32[]{:S(2)}) collective-permute-start(bf16[2,2,128,256]{3,2,0,1:T(8,128)(2,1)S(1)} %get-tuple-element.322), channel_id=1, source_target_pairs={{0,4},{4,8},{8,12},{12,0},{1,5},{5,9},{9,13},{13,1},{2,6},{6,10},{... | collective-permute-start | bytes 786440 | tf_op jit(solution)/shard_map/ppermute | solution.py:27
  133.4 240.9 %all-reduce.6.cloned.1.call-start = ((), (), s32[]{:S(2)}) async-start(), calls=%async_computation.3 | async-start | bytes 8388608 | tf_op jit(solution)/shard_map/psum | solution.py:15
  389.5 1.9 copy-start
  725.0 23.0 %all-to-all-start.1 = ((f32[4,1,65536]{2,1,0:T(1,128)}), f32[4,1,65536]{2,1,0:T(1,128)S(1)}, u32[]{:S(2)}, u32[]{:S(2)}) async-start(f32[4,1,65536]{2,1,0:T(1,128)} %reshape.847), calls=%async_computation.1 | async-start | bytes 2097152 | tf_op jit(solution)/shard_map/all_to_all | solution.py:168
Sparse Core Ops, SparseCore 0:
  133.5 82.9 all-reduce.3
  219.0 155.2 all-reduce.5
